TPU v7x, 32 devices: a whole 2x2x4 slice. The times are simulated.
32 devices in a mesh: geom: 2 (over x), edge: 4 (over y, core), mode: 4 (over z).
Axes of the slice: x: 2, y: 2, z: 4, core: 2. Of those that a mesh axis runs over, the one named last changes fastest.
Arguments:
- basis: bfloat16 [12288, 1024], P(('geom', 'edge'), 'mode'), parts along dimension 0, may hold values from -6 to 6
- motional: bfloat16 [4, 48, 16, 128, 128], P('geom', 'edge'), parts along dimension 0, may hold values from -0.0017089844 to 0.0017089844
- block_cols: int32 [96, 16], P(('geom', 'edge')), parts along dimension 0, may hold values from 0 to 47, as said below
- block_counts: int32 [96], P(('geom', 'edge')), parts along dimension 0, may hold values from 8 to 16, as said below
Outputs:
- reduced: float32 [4, 1024, 1024], P('geom', 'edge', 'mode'), parts along dimension 0
There are 2 independent parts, one for each index of `geom`. A program takes and returns all parts, laid end to end along the dimension named above; each array names one. Nothing has to cross between parts.
Inputs may be any that keep to these rules, and one draw needn't show every extreme that they name: `block_cols`: block row r's live slots hold distinct block columns within 12 blocks of r (at most r + 12, at least r - 12); slot 0 is r itself; slots at or past block_counts[r] hold r. block_counts[r] never exceeds the number of block columns within 12 blocks of r.
All inputs are finite; a program needn't handle non-finite values.
Results may differ from a plain program's by a relative error of at most 0.0029.
Values may be sent and summed in bfloat16 or wider, within the bound.
A program may use at most 64 MiB of HBM per device.

v0:
```python
import jax
import jax.numpy as jnp
from jax import lax
from jax.sharding import PartitionSpec as P


def padded(x, sides, width):
    for axis, dim in sides:
        size, length = (lax.axis_size(axis), x.shape[dim])
        up = [(i, (i + 1) % size) for i in range(size - 1)]
        down = [(j, i) for i, j in up]
        last = lax.slice_in_dim(x, length - width, length, axis=dim)
        initial = lax.slice_in_dim(x, 0, width, axis=dim)
        before = lax.ppermute(last, axis, up)
        after = lax.ppermute(initial, axis, down)
        x = jnp.concatenate([before, x, after], axis=dim)
    return x


def per_device(basis, motional, block_cols, block_counts):
    rows, cols_local = basis.shape
    nbr, nnz = block_cols.shape
    bsize = motional.shape[-1]
    extended = padded(basis, (("edge", 0),), nbr * bsize)
    tiles = extended.reshape(3 * nbr, bsize, cols_local)
    first_block = lax.axis_index("edge") * nbr
    local_cols = block_cols - first_block + nbr
    live = jnp.arange(nnz, dtype=jnp.int32)[None, :] < block_counts[:, None]
    picked = jnp.take(tiles, local_cols, axis=0)
    picked = jnp.where(live[:, :, None, None], picked, jnp.zeros_like(picked))
    work = jnp.einsum("qbkij,bkjm->qbim", motional, picked, preferred_element_type=jnp.float32)
    work = work.astype(jnp.bfloat16).reshape(2, rows, cols_local)
    partial_sum = jnp.einsum(
        "ri,qrj->qij",
        lax.all_gather(basis, "mode", axis=1, tiled=True),
        work,
        preferred_element_type=jnp.float32,
    )
    total = lax.psum(partial_sum, "edge")
    share = total.shape[1] // lax.axis_size("edge")
    return lax.dynamic_slice_in_dim(total, lax.axis_index("edge") * share, share, 1)


def solution(mesh):
    placed = (
        P(("geom", "edge"), "mode"),
        P("geom", "edge", None, None, None),
        P(("geom", "edge"), None),
        P(("geom", "edge")),
    )
    return jax.shard_map(
        per_device, mesh=mesh, in_specs=placed, out_specs=P("geom", "edge", "mode"), check_vma=False
    )
```

profile of v0, /device:TPU:0, one launch (start us, length us, event | category | flops | bytes accessed | tf_op | source)
XLA Modules:
  0.0 138.8 jit_solution(16012564998397765538)
XLA Ops:
  6.5 0.0 all-gather.2.cloned.1.call-start
  6.5 0.7 all-gather.2.cloned.1.call-update
  7.3 0.0 all-reduce.2.cloned.1.call-start
  7.3 2.4 %collective-permute-start = (bf16[1536,256]{1,0:T(8,128)(2,1)}, bf16[1536,256]{1,0:T(8,128)(2,1)S(1)}, u32[]{:S(2)}, u32[]{:S(2)}) collective-permute-start(bf16[1536,256]{1,0:T(8,128)(2,1)} %param.4), channel_id=1, source_target_pairs={{0,4},{4,8},{8,12},{1,5},{5,9},{9,13},{2,6},{6,10},{10,14},{3,7},{... | collective-permute-start | bytes 2359304 | tf_op jit(solution)/shard_map/ppermute | solution.py:14
  9.7 1.3 collective-permute-start.1
  11.0 0.8 compare_and_fusion
  11.8 0.1 reshape.36
  11.9 0.0 collective-permute-done
  11.9 4.4 %collective-permute-done.1 = bf16[1536,256]{1,0:T(8,128)(2,1)} collective-permute-done((bf16[1536,256]{1,0:T(8,128)(2,1)}, bf16[1536,256]{1,0:T(8,128)(2,1)}, u32[]{:S(2)}, u32[]{:S(2)}) %collective-permute-start.1) | collective-permute-done | bytes 786464 | tf_op jit(solution)/shard_map/ppermute | solution.py:15
  16.3 1.5 %pad_maximum_fusion = bf16[4608,256]{1,0:T(8,128)(2,1)S(1)} fusion(bf16[1536,256]{1,0:T(8,128)(2,1)} %collective-permute-done.1, bf16[1536,256]{1,0:T(8,128)(2,1)} %param.4, bf16[1536,256]{1,0:T(8,128)(2,1)S(1)} %collective-permute-done), kind=kLoop, calls=%fused_computation.13 | loop fusion | flops 7077888 | bytes 4718592 | tf_op jit(solution)/shard_map/concatenate | solution.py:16
  17.9 8.2 %gather_fusion = bf16[192,128,256]{2,1,0:T(8,128)(2,1)} fusion(bf16[36,128,256]{2,1,0:T(8,128)(2,1)S(1)} %bitcast.27, s32[1024]{0:T(1024)S(1)} %pad_clamp_fusion), kind=kCustom, calls=%fused_computation | custom fusion | bytes 25166592 | tf_op jit(solution)/shard_map/jit(_take)/gather | solution.py:29
  26.1 10.5 %fusion.18 = bf16[2,12,128,256]{3,2,0,1:T(8,128)(2,1)S(1)} fusion(bf16[2,12,16,128,128]{4,3,2,1,0:T(8,128)(2,1)} %param.5, bf16[12,16,128,256]{3,2,1,0:T(8,128)(2,1)} %bitcast.28, pred[12,16]{1,0:T(8,128)(4,1)S(1)} %get-tuple-element.5, pred[12,16]{1,0:T(8,128)(4,1)S(1)} %get-tuple-element.7), kind=kOutput, calls=%fused_computation.15 | convolution fusion | flops 3234594816 | bytes 26739072 | tf_op jit(solution)/shard_map/qbkij,bkjm->qbim/dot_general | solution.py:31
  36.5 0.1 copy.8
  36.7 38.4 %all-gather.2.cloned.1.call-done = bf16[1536,1024]{1,0:T(8,128)(2,1)} async-done(((bf16[1536,256]{1,0:T(8,128)(2,1)}), bf16[1536,1024]{1,0:T(8,128)(2,1)}) %all-gather.2.cloned.1.call-update) | async-done | bytes 3145744 | tf_op jit(solution)/shard_map/all_gather | solution.py:35
  75.1 5.0 %fusion.15 = f32[2,1024,256]{1,2,0:T(8,128)} fusion(bf16[2,1536,256]{2,1,0:T(8,128)(2,1)S(1)} %bitcast.29, bf16[1536,1024]{1,0:T(8,128)(2,1)} %all-gather.2.cloned.1.call-done), kind=kOutput, calls=%fused_computation.14 | convolution fusion | flops 1610612736 | bytes 6815744 | tf_op jit(solution)/shard_map/ri,qrj->qij/dot_general | solution.py:33
  80.1 0.0 all-reduce.2.cloned.1.call-update
  80.2 49.7 %all-reduce.2.cloned.1.call-done = f32[2,1024,256]{1,2,0:T(8,128)} async-done(((f32[2,1024,256]{1,2,0:T(8,128)}), f32[2,1024,256]{1,2,0:T(8,128)}) %all-reduce.2.cloned.1.call-update) | async-done | bytes 2097168 | tf_op jit(solution)/shard_map/psum | solution.py:39
  129.9 1.1 constant_dynamic-slice_fusion
  130.9 1.0 copy.10
  (1 shorter events, 0.0 us)
Async XLA Ops:
  6.5 68.5 %all-gather.2.cloned.1.call-start = ((), (), s32[]{:S(2)}) async-start(), calls=%async_computation | async-start | bytes 3932160 | tf_op jit(solution)/shard_map/all_gather | solution.py:35
  7.3 122.6 %all-reduce.2.cloned.1.call-start = ((), (), s32[]{:S(2)}) async-start(), calls=%async_computation.1 | async-start | bytes 4194304 | tf_op jit(solution)/shard_map/psum | solution.py:39
  7.3 4.6 %collective-permute-start = (bf16[1536,256]{1,0:T(8,128)(2,1)}, bf16[1536,256]{1,0:T(8,128)(2,1)S(1)}, u32[]{:S(2)}, u32[]{:S(2)}) collective-permute-start(bf16[1536,256]{1,0:T(8,128)(2,1)} %param.4), channel_id=1, source_target_pairs={{0,4},{4,8},{8,12},{1,5},{5,9},{9,13},{2,6},{6,10},{10,14},{3,7},{... | collective-permute-start | bytes 2359304 | tf_op jit(solution)/shard_map/ppermute | solution.py:14
  9.7 6.6 %collective-permute-start.1 = (bf16[1536,256]{1,0:T(8,128)(2,1)}, bf16[1536,256]{1,0:T(8,128)(2,1)}, u32[]{:S(2)}, u32[]{:S(2)}) collective-permute-start(bf16[1536,256]{1,0:T(8,128)(2,1)} %param.4), channel_id=1, source_target_pairs={{4,0},{8,4},{12,8},{5,1},{9,5},{13,9},{6,2},{10,6},{14,10},{7,3},{... | collective-permute-start | bytes 2359304 | tf_op jit(solution)/shard_map/ppermute | solution.py:15
Sparse Core Ops, SparseCore 0:
  8.9 66.1 all-gather.1
  80.3 49.5 all-reduce.1
where the time goes:
time: 139 us
  waiting for transfers between devices  93.2 us (67%)
  matrix products  15.5 us (11%)
  between operations  13.5 us (10%)
  local copies, waits for them, and re-layouts  10.5 us (8%)
  starting transfers between devices  3.74 us (3%)
  other arithmetic  2.31 us (2%)
    psum x1, waiting for transfers between devices, per_device(): total = lax.psum(partial_sum, 'edge')  49.7 us
    all_gather x1, waiting for transfers between devices, per_device(): lax.all_gather(basis, 'mode', axis=1, tiled=True)  38.4 us
    dot_general x1, matrix products, per_device(): jnp.einsum('qbkij,bkjm->qbim', motional, picked, preferred_element_type=j...  10.5 us
    gather x1, local copies, waits for them, and re-layouts, per_device(): picked = jnp.take(tiles, local_cols, axis=0)  8.2 us
    dot_general x1, matrix products, per_device(): jnp.einsum('ri,qrj->qij', lax.all_gather(basis, 'mode', axis=1, tiled=Tru...  5.05 us
    ppermute x1, waiting for transfers between devices, padded(): after = lax.ppermute(initial, axis, down)  4.43 us
  transfers between devices with their start and end apart: 4, of which 3 were waited for; matrix products, arithmetic and copies ran while one was open for 15% of the time, Pallas kernels for 0%

commit v1 on v0

--- a/solution.py
+++ b/solution.py
@@ -2,6 +2,27 @@
 import jax.numpy as jnp
 from jax import lax
 from jax.sharding import PartitionSpec as P
+
+
+def _advance_spot(row_data, ndim_at):
+    row_data = jnp.moveaxis(row_data, 0, ndim_at)
+    seen_now = row_data.shape
+    return row_data.reshape(
+        *seen_now[:ndim_at], seen_now[ndim_at] * seen_now[ndim_at + 1], *seen_now[ndim_at + 2 :]
+    )
+
+
+def expand_lanes_over_axis(values, ax_name, k_dim, original, on_dim=1):
+    low, wide_out, latest = (lax.axis_size(ax_name), lax.axis_index(ax_name), values.shape[k_dim])
+    xs_all = []
+    g_now = values
+    items = [(h, (h + 1) % low) for h in range(low)]
+    for u in range(low):
+        tmp = g_now if u == low - 1 else lax.ppermute(g_now, ax_name, items)
+        xs_all.append(original(g_now, (wide_out - u) % low * latest))
+        g_now = tmp
+    xs_all = jnp.stack(xs_all, axis=0)[(wide_out - jnp.arange(low)) % low]
+    return _advance_spot(xs_all, on_dim)
 
 
 def padded(x, sides, width):
@@ -30,11 +51,13 @@
     picked = jnp.where(live[:, :, None, None], picked, jnp.zeros_like(picked))
     work = jnp.einsum("qbkij,bkjm->qbim", motional, picked, preferred_element_type=jnp.float32)
     work = work.astype(jnp.bfloat16).reshape(2, rows, cols_local)
-    partial_sum = jnp.einsum(
-        "ri,qrj->qij",
-        lax.all_gather(basis, "mode", axis=1, tiled=True),
-        work,
-        preferred_element_type=jnp.float32,
+    partial_sum = expand_lanes_over_axis(
+        basis,
+        "mode",
+        1,
+        lambda own_block, start: jnp.einsum(
+            "ri,qrj->qij", own_block, work, preferred_element_type=jnp.float32
+        ),
     )
     total = lax.psum(partial_sum, "edge")
     share = total.shape[1] // lax.axis_size("edge")

time: 139 us -> 139 us (level)
  waiting for transfers between devices: 93.2 us -> 86.7 us
  local copies, waits for them, and re-layouts: 10.5 us -> 15.2 us
  starting transfers between devices: 3.74 us -> 6.43 us
  matrix products: 15.5 us -> 14 us
    all_gather x1 -> x0, waiting for transfers between devices: 38.4 us -> none  [per_device(): lax.all_gather(basis, 'mode', axis=1, tiled=True)]
    ppermute x0 -> x3, waiting for transfers between devices: none -> 33 us  [expand_lanes_over_axis(): tmp = g_now if u == low - 1 else lax.ppermute(g_now, ax_name, items)]
    transpose x0 -> x1, local copies, waits for them, and re-layouts: none -> 2.95 us  [_advance_spot(): row_data = jnp.moveaxis(row_data, 0, ndim_at)]
    ppermute x0 -> x3, starting transfers between devices: none -> 2.74 us  [expand_lanes_over_axis(): tmp = g_now if u == low - 1 else lax.ppermute(g_now, ax_name, items)]
    ppermute x1, waiting for transfers between devices: 4.43 us -> 1.95 us  [padded(): after = lax.ppermute(initial, axis, down)]
    psum x1, waiting for transfers between devices: 49.7 us -> 51.8 us  [per_device(): total = lax.psum(partial_sum, 'edge')]
    gather x0 -> x1, local copies, waits for them, and re-layouts: none -> 1.99 us  [expand_lanes_over_axis(): xs_all = jnp.stack(xs_all, axis=0)[(wide_out - jnp.arange(low)) % low]]
    dot_general x1 -> x4, matrix products: 5.05 us -> 3.57 us  [per_device(): jnp.einsum('ri,qrj->qij', own_block, work, preferred_element_type=jnp.flo...]
  transfers between devices with their start and end apart: 4 -> 6, of which waited for: 3 -> 5; matrix products, arithmetic and copies ran while one was open for 15% -> 17% of each run, Pallas kernels for 0% -> 0%
where the time goes in v1:
time: 139 us; the launch traced here: 138 us
  waiting for transfers between devices  86.7 us (62%)
  local copies, waits for them, and re-layouts  15.2 us (11%)
  matrix products  14 us (10%)
  between operations  13.5 us (10%)
  starting transfers between devices  6.43 us (5%)
  other arithmetic  2.55 us (2%)
    psum x1, waiting for transfers between devices, per_device(): total = lax.psum(partial_sum, 'edge')  51.8 us
    ppermute x3, waiting for transfers between devices, expand_lanes_over_axis(): tmp = g_now if u == low - 1 else lax.ppermute(g_now, ax_name, items)  33 us
    dot_general x1, matrix products, per_device(): jnp.einsum('qbkij,bkjm->qbim', motional, picked, preferred_element_type=j...  10.4 us
    gather x1, local copies, waits for them, and re-layouts, per_device(): picked = jnp.take(tiles, local_cols, axis=0)  8.19 us
    dot_general x4, matrix products, per_device(): jnp.einsum('ri,qrj->qij', own_block, work, preferred_element_type=jnp.flo...  3.57 us
    transpose x1, local copies, waits for them, and re-layouts, _advance_spot(): row_data = jnp.moveaxis(row_data, 0, ndim_at)  2.95 us
  transfers between devices with their start and end apart: 6, of which 5 were waited for; matrix products, arithmetic and copies ran while one was open for 17% of the time, Pallas kernels for 0%

profile of v1, /device:TPU:0, one launch (start us, length us, event | category | flops | bytes accessed | tf_op | source)
XLA Modules:
  0.0 138.4 jit_solution(8554068915400932479)
XLA Ops:
  6.5 2.4 %collective-permute-start = (bf16[1536,256]{1,0:T(8,128)(2,1)}, bf16[1536,256]{1,0:T(8,128)(2,1)S(1)}, u32[]{:S(2)}, u32[]{:S(2)}) collective-permute-start(bf16[1536,256]{1,0:T(8,128)(2,1)} %param.4), channel_id=1, source_target_pairs={{0,4},{4,8},{8,12},{1,5},{5,9},{9,13},{2,6},{6,10},{10,14},{3,7},{... | collective-permute-start | bytes 2359304 | tf_op jit(solution)/shard_map/ppermute | solution.py:35
  8.9 1.3 collective-permute-start.1
  10.2 2.5 %collective-permute-start.2 = (bf16[1536,256]{1,0:T(8,128)(2,1)}, bf16[1536,256]{1,0:T(8,128)(2,1)}, u32[]{:S(2)}, u32[]{:S(2)}) collective-permute-start(bf16[1536,256]{1,0:T(8,128)(2,1)} %param.4), channel_id=1, source_target_pairs={{0,1},{1,2},{2,3},{3,0},{4,5},{5,6},{6,7},{7,4},{8,9},{9,10},{10,1... | collective-permute-start | bytes 2359304 | tf_op jit(solution)/shard_map/ppermute | solution.py:21
  12.7 0.8 compare_and_fusion
  13.5 0.1 reshape.89
  13.6 2.0 %collective-permute-done.1 = bf16[1536,256]{1,0:T(8,128)(2,1)} collective-permute-done((bf16[1536,256]{1,0:T(8,128)(2,1)}, bf16[1536,256]{1,0:T(8,128)(2,1)}, u32[]{:S(2)}, u32[]{:S(2)}) %collective-permute-start.1) | collective-permute-done | bytes 786464 | tf_op jit(solution)/shard_map/ppermute | solution.py:36
  15.6 1.5 %pad_maximum_fusion = bf16[4608,256]{1,0:T(8,128)(2,1)S(1)} fusion(bf16[1536,256]{1,0:T(8,128)(2,1)} %collective-permute-done.1, bf16[1536,256]{1,0:T(8,128)(2,1)} %param.4, bf16[1536,256]{1,0:T(8,128)(2,1)S(1)} %collective-permute-done), kind=kLoop, calls=%fused_computation.12 | loop fusion | flops 7077888 | bytes 4718592 | tf_op jit(solution)/shard_map/concatenate | solution.py:37
  17.1 8.2 %gather_fusion = bf16[192,128,256]{2,1,0:T(8,128)(2,1)} fusion(bf16[36,128,256]{2,1,0:T(8,128)(2,1)S(1)} %bitcast.55, s32[1024]{0:T(1024)S(1)} %pad_clamp_fusion.1), kind=kCustom, calls=%fused_computation | custom fusion | bytes 25166592 | tf_op jit(solution)/shard_map/jit(_take)/gather | solution.py:50
  25.3 6.4 %collective-permute-done.2 = bf16[1536,256]{1,0:T(8,128)(2,1)} collective-permute-done((bf16[1536,256]{1,0:T(8,128)(2,1)}, bf16[1536,256]{1,0:T(8,128)(2,1)}, u32[]{:S(2)}, u32[]{:S(2)}) %collective-permute-start.2) | collective-permute-done | bytes 786464 | tf_op jit(solution)/shard_map/ppermute | solution.py:21
  31.7 0.3 collective-permute-start.3
  32.0 10.4 %fusion.13 = bf16[2,12,128,256]{3,2,0,1:T(8,128)(2,1)S(1)} fusion(bf16[2,12,16,128,128]{4,3,2,1,0:T(8,128)(2,1)} %param.5, bf16[12,16,128,256]{3,2,1,0:T(8,128)(2,1)} %bitcast.56, pred[12,16]{1,0:T(8,128)(4,1)S(1)} %get-tuple-element.5, pred[12,16]{1,0:T(8,128)(4,1)S(1)} %get-tuple-element.7), kind=kOutput, calls=%fused_computation.14 | convolution fusion | flops 3234594816 | bytes 26739072 | tf_op jit(solution)/shard_map/qbkij,bkjm->qbim/dot_general | solution.py:52
  42.4 0.1 copy.7
  42.5 8.9 %collective-permute-done.3 = bf16[1536,256]{1,0:T(8,128)(2,1)S(1)} collective-permute-done((bf16[1536,256]{1,0:T(8,128)(2,1)}, bf16[1536,256]{1,0:T(8,128)(2,1)S(1)}, u32[]{:S(2)}, u32[]{:S(2)}) %collective-permute-start.3) | collective-permute-done | bytes 786464 | tf_op jit(solution)/shard_map/ppermute | solution.py:21
  51.4 0.6 convolution_bitcast_fusion.3
  52.1 1.7 %convolution_bitcast_fusion.2 = f32[1,2,256,256]{2,3,1,0:T(8,128)S(1)} fusion(bf16[2,1536,256]{2,1,0:T(8,128)(2,1)S(1)} %bitcast.60, bf16[1536,256]{1,0:T(8,128)(2,1)} %collective-permute-done.2), kind=kOutput, calls=%fused_computation.17 | convolution fusion | flops 402653184 | bytes 2883584 | tf_op jit(solution)/shard_map/ri,qrj->qij/dot_general | solution.py:58
  53.8 0.6 convolution_bitcast_fusion.1
  54.4 17.6 %collective-permute-done.4 = bf16[1536,256]{1,0:T(8,128)(2,1)S(1)} collective-permute-done((bf16[1536,256]{1,0:T(8,128)(2,1)S(1)}, bf16[1536,256]{1,0:T(8,128)(2,1)S(1)}, u32[]{:S(2)}, u32[]{:S(2)}) %collective-permute-start.4) | collective-permute-done | bytes 786464 | tf_op jit(solution)/shard_map/ppermute | solution.py:21
  72.1 0.6 convolution_bitcast_fusion
  72.7 0.2 pad_maximum_fusion.1
  72.9 2.0 %gather_fusion.1 = f32[4,2,256,256]{2,3,1,0:T(8,128)} fusion(f32[4,2,256,256]{2,3,1,0:T(8,128)S(1)} %pad_maximum_fusion.1, s32[1024]{0:T(1024)S(1)} %pad_clamp_fusion), kind=kCustom, calls=%fused_computation.1 | custom fusion | bytes 4194320 | tf_op jit(solution)/shard_map/gather | solution.py:24
  74.9 2.9 %copy.12 = f32[2,4,256,256]{3,2,1,0:T(8,128)} copy(f32[2,4,256,256]{2,3,0,1:T(8,128)} %bitcast.58) | data formatting | bytes 4194304 | tf_op jit(solution)/shard_map/transpose | solution.py:8
  77.8 0.0 all-reduce.2.cloned.1.call-update
  77.9 51.8 %all-reduce.2.cloned.1.call-done = f32[2,1024,256]{2,1,0:T(8,128)} async-done(((f32[2,1024,256]{2,1,0:T(8,128)}), f32[2,1024,256]{2,1,0:T(8,128)}) %all-reduce.2.cloned.1.call-update) | async-done | bytes 2097168 | tf_op jit(solution)/shard_map/psum | solution.py:62
  129.7 1.9 %constant_dynamic-slice_fusion = f32[2,256,256]{2,1,0:T(8,128)} fusion(f32[2,1024,256]{2,1,0:T(8,128)} %all-reduce.2.cloned.1.call-done, s32[]{:T(128)S(6)} %select_n.45), kind=kLoop, calls=%fused_computation.34 | loop fusion | bytes 1048580 | tf_op jit(solution)/shard_map/dynamic_slice | solution.py:64
  (8 shorter events, 0.0 us)
Async XLA Ops:
  6.5 123.2 %all-reduce.2.cloned.1.call-start = ((), (), s32[]{:S(2)}) async-start(), calls=%async_computation | async-start | bytes 4194304 | tf_op jit(solution)/shard_map/psum | solution.py:62
  6.5 7.1 %collective-permute-start = (bf16[1536,256]{1,0:T(8,128)(2,1)}, bf16[1536,256]{1,0:T(8,128)(2,1)S(1)}, u32[]{:S(2)}, u32[]{:S(2)}) collective-permute-start(bf16[1536,256]{1,0:T(8,128)(2,1)} %param.4), channel_id=1, source_target_pairs={{0,4},{4,8},{8,12},{1,5},{5,9},{9,13},{2,6},{6,10},{10,14},{3,7},{... | collective-permute-start | bytes 2359304 | tf_op jit(solution)/shard_map/ppermute | solution.py:35
  8.9 6.6 %collective-permute-start.1 = (bf16[1536,256]{1,0:T(8,128)(2,1)}, bf16[1536,256]{1,0:T(8,128)(2,1)}, u32[]{:S(2)}, u32[]{:S(2)}) collective-permute-start(bf16[1536,256]{1,0:T(8,128)(2,1)} %param.4), channel_id=1, source_target_pairs={{4,0},{8,4},{12,8},{5,1},{9,5},{13,9},{6,2},{10,6},{14,10},{7,3},{... | collective-permute-start | bytes 2359304 | tf_op jit(solution)/shard_map/ppermute | solution.py:36
  10.2 21.4 %collective-permute-start.2 = (bf16[1536,256]{1,0:T(8,128)(2,1)}, bf16[1536,256]{1,0:T(8,128)(2,1)}, u32[]{:S(2)}, u32[]{:S(2)}) collective-permute-start(bf16[1536,256]{1,0:T(8,128)(2,1)} %param.4), channel_id=1, source_target_pairs={{0,1},{1,2},{2,3},{3,0},{4,5},{5,6},{6,7},{7,4},{8,9},{9,10},{10,1... | collective-permute-start | bytes 2359304 | tf_op jit(solution)/shard_map/ppermute | solution.py:21
  31.7 19.8 %collective-permute-start.3 = (bf16[1536,256]{1,0:T(8,128)(2,1)}, bf16[1536,256]{1,0:T(8,128)(2,1)S(1)}, u32[]{:S(2)}, u32[]{:S(2)}) collective-permute-start(bf16[1536,256]{1,0:T(8,128)(2,1)} %collective-permute-done.2), channel_id=1, source_target_pairs={{0,1},{1,2},{2,3},{3,0},{4,5},{5,6},{6,7},{7,4},{8,9},{9,10},{10,1... | collective-permute-start | bytes 2359304 | tf_op jit(solution)/shard_map/ppermute | solution.py:21
  42.4 9.0 %copy-start = (bf16[1536,256]{1,0:T(8,128)(2,1)S(1)}, bf16[1536,256]{1,0:T(8,128)(2,1)}, u32[]{:S(2)}) copy-start(bf16[1536,256]{1,0:T(8,128)(2,1)} %param.4) | copy-start | bytes 2359300
  51.4 20.6 %collective-permute-start.4 = (bf16[1536,256]{1,0:T(8,128)(2,1)S(1)}, bf16[1536,256]{1,0:T(8,128)(2,1)S(1)}, u32[]{:S(2)}, u32[]{:S(2)}) collective-permute-start(bf16[1536,256]{1,0:T(8,128)(2,1)S(1)} %collective-permute-done.3), channel_id=1, source_target_pairs={{0,1},{1,2},{2,3},{3,0},{4,5},{5,6},{6,7},{7,4},{8,9},{9,10},{10,1... | collective-permute-start | bytes 2359304 | tf_op jit(solution)/shard_map/ppermute | solution.py:21
Sparse Core Ops, SparseCore 0:
  78.0 51.6 all-reduce.1
